TPU v7x, 32 devices: a whole 2x2x4 slice. The times are simulated.
32 devices in a mesh: row: 4 (over y, core), col: 8 (over z, x).
Axes of the slice: x: 2, y: 2, z: 4, core: 2. Of those that a mesh axis runs over, the one named last changes fastest.
Arguments:
- tokens: bfloat16 [1024, 6144], P('row', 'col'), may hold values from -6 to 6
- cotangent: bfloat16 [1024, 6144], P('row', 'col'), may hold values from -6 to 6
- w_expand: bfloat16 [6144, 12288], P('row', 'col'), may hold values from -0.078125 to 0.078125
- w_reduce: bfloat16 [6144, 12288], P('row', 'col'), may hold values from -0.0546875 to 0.0546875
- expand_mean: bfloat16 [6144, 12288], P('row', 'col'), may hold values from -1 to 1
- expand_mean_scale: float32 [24, 12288], P('row', 'col'), may hold values from 4 to 16
- expand_var: bfloat16 [6144, 12288], P('row', 'col'), may hold values from 0.049804688 to 1
- expand_var_scale: float32 [24, 12288], P('row', 'col'), may hold values from 4 to 16
- reduce_mean: bfloat16 [6144, 12288], P('row', 'col'), may hold values from -1 to 1
- reduce_mean_scale: float32 [24, 12288], P('row', 'col'), may hold values from 4 to 16
- reduce_var: bfloat16 [6144, 12288], P('row', 'col'), may hold values from 0.049804688 to 1
- reduce_var_scale: float32 [24, 12288], P('row', 'col'), may hold values from 4 to 16
Outputs:
- grad_tokens: bfloat16 [1024, 6144], P('row', 'col')
- new_expand: bfloat16 [6144, 12288], P('row', 'col')
- expand_mean_next: bfloat16 [6144, 12288], P('row', 'col')
- expand_mean_scale_next: float32 [24, 12288], P('row', 'col')
- expand_var_next: bfloat16 [6144, 12288], P('row', 'col')
- expand_var_scale_next: float32 [24, 12288], P('row', 'col')
- new_reduce: bfloat16 [6144, 12288], P('row', 'col')
- reduce_mean_next: bfloat16 [6144, 12288], P('row', 'col')
- reduce_mean_scale_next: float32 [24, 12288], P('row', 'col')
- reduce_var_next: bfloat16 [6144, 12288], P('row', 'col')
- reduce_var_scale_next: float32 [24, 12288], P('row', 'col')
All inputs are finite; a program needn't handle non-finite values.
Results may differ from a plain program's by a relative error of at most 0.0049.
Values may be sent and summed in bfloat16 or wider, within the bound.
A program may use at most 192 MiB of HBM per device.

v0:
```python
import jax
import jax.numpy as jnp
from jax import lax
from jax.sharding import PartitionSpec as P

STEP = 10


beta_one = 0.9
beta_two = 0.999
adam_eps = 1e-08
learn_rate = 0.001
decay_rate = 0.1
scale_eps = 1e-06


def gelu_pair(pre_act):
    cdf_part = 0.5 * (1.0 + lax.erf(pre_act * 0.7071067811865476))
    slope = cdf_part + pre_act * jnp.exp(-0.5 * pre_act * pre_act) * 0.3989422804014327
    return (pre_act * cdf_part, slope)


def spread_scale(values, scale):
    blocks = scale.shape[0]
    shaped = values.reshape(blocks, values.shape[0] // blocks, values.shape[1])
    return (shaped * scale[:, None, :]).reshape(values.shape)


def block_max(values, blocks):
    shaped = values.reshape(blocks, values.shape[0] // blocks, values.shape[1])
    return jnp.max(jnp.abs(shaped), axis=1) + scale_eps


def adam_step(weight, grad_w, mean_q, mean_scale, var_q, var_scale):
    blocks = mean_scale.shape[0]
    mean_new = (
        beta_one * spread_scale(mean_q.astype(jnp.float32), mean_scale) + (1.0 - beta_one) * grad_w
    )
    var_new = (
        beta_two * spread_scale(var_q.astype(jnp.float32), var_scale)
        + (1.0 - beta_two) * grad_w * grad_w
    )
    mean_hat = mean_new / (1.0 - beta_one**STEP)
    var_hat = var_new / (1.0 - beta_two**STEP)
    old_weight = weight.astype(jnp.float32)
    new_weight = (
        old_weight
        - learn_rate * (mean_hat / (jnp.sqrt(var_hat) + adam_eps) + decay_rate * old_weight)
    ).astype(jnp.bfloat16)
    mean_scale_next = block_max(mean_new, blocks)
    var_scale_next = block_max(var_new, blocks)
    mean_next = spread_scale(mean_new, 1.0 / mean_scale_next).astype(jnp.bfloat16)
    var_next = spread_scale(var_new, 1.0 / var_scale_next).astype(jnp.bfloat16)
    return (new_weight, mean_next, mean_scale_next, var_next, var_scale_next)


def contract_first(left, right):
    return lax.dot_general(
        left, right, (((0,), (0,)), ((), ())), preferred_element_type=jnp.float32
    )


def local(
    tokens,
    cotangent,
    w_expand,
    w_reduce,
    expand_mean,
    expand_mean_scale,
    expand_var,
    expand_var_scale,
    reduce_mean,
    reduce_mean_scale,
    reduce_var,
    reduce_var_scale,
):
    token_rows, cot_rows = (
        lax.all_gather(tokens, "col", axis=1, tiled=True),
        lax.all_gather(cotangent, "col", axis=1, tiled=True),
    )
    input_whole, cot_whole = (
        lax.all_to_all(token_rows, "row", split_axis=1, concat_axis=0, tiled=True),
        lax.all_to_all(cot_rows, "row", split_axis=1, concat_axis=0, tiled=True),
    )
    up_panel = lax.all_gather(w_expand, "row", axis=0, tiled=True)
    cot_part = cot_whole
    act_grad = lax.psum_scatter(
        jnp.dot(cot_part, w_reduce, preferred_element_type=jnp.float32),
        "row",
        scatter_dimension=0,
        tiled=True,
    )
    pre_act = jnp.dot(token_rows, up_panel, preferred_element_type=jnp.float32)
    activated, slope = gelu_pair(pre_act)
    activated = activated.astype(jnp.bfloat16)
    pre_grad = (act_grad * slope).astype(jnp.bfloat16)
    grad_cols = lax.psum_scatter(
        lax.dot_general(
            up_panel, pre_grad, (((1,), (1,)), ((), ())), preferred_element_type=jnp.float32
        ),
        "col",
        scatter_dimension=0,
        tiled=True,
    )
    grad_tokens = grad_cols.T.astype(jnp.bfloat16)
    cot_part = cot_whole
    grad_expand = contract_first(input_whole, lax.all_gather(pre_grad, "row", axis=0, tiled=True))
    grad_reduce = contract_first(cot_part, lax.all_gather(activated, "row", axis=0, tiled=True))
    first = adam_step(
        w_expand, grad_expand, expand_mean, expand_mean_scale, expand_var, expand_var_scale
    )
    second = adam_step(
        w_reduce, grad_reduce, reduce_mean, reduce_mean_scale, reduce_var, reduce_var_scale
    )
    return (
        grad_tokens,
        first[0],
        first[1],
        first[2],
        first[3],
        first[4],
        second[0],
        second[1],
        second[2],
        second[3],
        second[4],
    )


def solution(mesh):
    placed = (
        P("row", "col"),
        P("row", "col"),
        P("row", "col"),
        P("row", "col"),
        P("row", "col"),
        P("row", "col"),
        P("row", "col"),
        P("row", "col"),
        P("row", "col"),
        P("row", "col"),
        P("row", "col"),
        P("row", "col"),
    )
    return jax.shard_map(
        local,
        mesh=mesh,
        in_specs=placed,
        out_specs=(
            P("row", "col"),
            P("row", "col"),
            P("row", "col"),
            P("row", "col"),
            P("row", "col"),
            P("row", "col"),
            P("row", "col"),
            P("row", "col"),
            P("row", "col"),
            P("row", "col"),
            P("row", "col"),
        ),
        check_vma=False,
    )
```

profile of v0, /device:TPU:0, one launch (start us, length us, event | category | flops | bytes accessed | tf_op | source)
XLA Modules:
  0.0 538.4 jit_solution(396747935477568428)
XLA Ops:
  7.2 0.0 all-gather.6.cloned.1.call-start
  7.2 1.9 copy.23
  9.1 0.0 all-gather.6.cloned.1.call-update
  9.2 0.0 all-gather.8.cloned.1.call-start
  9.2 1.9 copy.25
  11.1 0.0 all-gather.8.cloned.1.call-update
  11.2 0.0 reduce-scatter.3.cloned.1.call-start
  11.2 62.7 %all-gather.6.cloned.1.call-done = bf16[256,6144]{0,1:T(8,128)(2,1)} async-done(((bf16[256,768]{0,1:T(8,128)(2,1)}), bf16[256,6144]{0,1:T(8,128)(2,1)}) %all-gather.6.cloned.1.call-update) | async-done | bytes 3145744 | tf_op jit(solution)/shard_map/all_gather | solution.py:79
  73.9 40.6 %all_to_all.38 = bf16[256,4,1536]{0,2,1:T(8,128)(2,1)S(1)} all-to-all(bf16[256,4,1536]{0,2,1:T(8,128)(2,1)} %bitcast.134), channel_id=1, replica_groups=mesh['row'=4,'col'=8] {'row'}, dimensions={1} | all-to-all | bytes 6291456 | tf_op jit(solution)/shard_map/all_to_all | solution.py:83
  114.5 2.8 copy.24
  117.3 9.7 %fusion.28 = f32[1024,1536]{1,0:T(8,128)} fusion(bf16[1024,1536]{1,0:T(8,128)(2,1)} %bitcast.131, bf16[1536,1536]{1,0:T(8,128)(2,1)} %param.15), kind=kOutput, calls=%fused_computation.57 | convolution fusion | flops 4831838208 | bytes 14155776 | tf_op jit(solution)/shard_map/dot_general | solution.py:88
  127.0 0.0 reduce-scatter.3.cloned.1.call-update
  127.1 0.0 all-gather.10.cloned.1.call-start
  127.1 0.5 all-gather.10.cloned.1.call-update
  127.6 0.0 all-gather.12.cloned.1.call-start
  127.7 8.1 %all-gather.8.cloned.1.call-done = bf16[256,6144]{0,1:T(8,128)(2,1)} async-done(((bf16[256,768]{0,1:T(8,128)(2,1)}), bf16[256,6144]{0,1:T(8,128)(2,1)}) %all-gather.8.cloned.1.call-update) | async-done | bytes 3145744 | tf_op jit(solution)/shard_map/all_gather | solution.py:78
  135.8 59.6 %reduce-scatter.3.cloned.1.call-done = f32[256,1536]{1,0:T(8,128)} async-done(((f32[1024,1536]{1,0:T(8,128)}), f32[256,1536]{1,0:T(8,128)}) %reduce-scatter.3.cloned.1.call-update) | async-done | bytes 1572880 | tf_op jit(solution)/shard_map/reduce_scatter | solution.py:87
  195.4 121.6 %all-gather.10.cloned.1.call-done = bf16[6144,1536]{1,0:T(8,128)(2,1)} async-done(((bf16[1536,1536]{1,0:T(8,128)(2,1)}), bf16[6144,1536]{1,0:T(8,128)(2,1)}) %all-gather.10.cloned.1.call-update) | async-done | bytes 18874384 | tf_op jit(solution)/shard_map/all_gather | solution.py:85
  316.9 11.4 %multiply_convert_fusion = (bf16[256,1536]{1,0:T(8,128)(2,1)}, bf16[256,1536]{1,0:T(8,128)(2,1)}) fusion(f32[256,1536]{1,0:T(8,128)} %reduce-scatter.3.cloned.1.call-done, bf16[256,6144]{0,1:T(8,128)(2,1)} %all-gather.8.cloned.1.call-done, bf16[6144,1536]{1,0:T(8,128)(2,1)} %all-gather.10.cloned.1.call-done), kind=kOutput, calls=%fused_computation.42 | convolution fusion | flops 4836556800 | bytes 25165824 | tf_op jit(solution)/shard_map/dot_general | solution.py:93
  328.4 0.0 all-gather.12.cloned.1.call-update
  328.4 0.0 all-gather.14.cloned.1.call-start
  328.4 0.5 all-gather.14.cloned.1.call-update
  329.0 0.0 copy-start
  329.0 0.0 reduce-scatter.5.cloned.1.call-start
  329.0 11.5 %convolution_bitcast_fusion = f32[6144,256]{0,1:T(8,128)} fusion(bf16[256,1536]{1,0:T(8,128)(2,1)} %get-tuple-element.26, bf16[6144,1536]{1,0:T(8,128)(2,1)} %all-gather.10.cloned.1.call-done), kind=kOutput, calls=%fused_computation.34 | convolution fusion | flops 4831838208 | bytes 25952256 | tf_op jit(solution)/shard_map/dot_general | solution.py:98
  340.5 0.0 reduce-scatter.5.cloned.1.call-update
  340.6 0.0 copy-done
  340.6 59.8 %all_to_all.39 = bf16[256,4,1536]{0,2,1:T(8,128)(2,1)} all-to-all(bf16[256,4,1536]{0,2,1:T(8,128)(2,1)S(1)} %bitcast.128), channel_id=1, replica_groups=mesh['row'=4,'col'=8] {'row'}, dimensions={1} | all-to-all | bytes 6291456 | tf_op jit(solution)/shard_map/all_to_all | solution.py:82
  400.4 3.2 copy.26
  403.6 0.0 all-gather.12.cloned.1.call-done
  403.6 12.2 %fusion.27 = (f32[1536,1536]{1,0:T(8,128)}, f32[1536,1536]{0,1:T(8,128)}) fusion(f32[6,1536]{1,0:T(8,128)S(1)} %copy-done.5, bf16[1536,1536]{1,0:T(8,128)(2,1)} %param.18, bf16[1024,1536]{1,0:T(8,128)(2,1)} %all-gather.12.cloned.1.call-done, bf16[1024,1536]{1,0:T(8,128)(2,1)S(1)} %bitcast.133), kind=kOutput, calls=%fused_computation.56 | convolution fusion | flops 4848353280 | bytes 29921280 | tf_op jit(solution)/shard_map/dot_general | solution.py:58
  415.9 5.1 reduce_max.37
  421.0 0.0 all-gather.14.cloned.1.call-done
  421.0 0.0 copy-done.1
  421.0 12.3 %fusion.26 = (f32[1536,1536]{1,0:T(8,128)}, f32[1536,1536]{0,1:T(8,128)}) fusion(f32[6,1536]{1,0:T(8,128)S(1)} %copy-done.4, bf16[1536,1536]{1,0:T(8,128)(2,1)} %param.22, bf16[1024,1536]{1,0:T(8,128)(2,1)} %all-gather.14.cloned.1.call-done, bf16[1024,1536]{1,0:T(8,128)(2,1)S(1)} %bitcast.132), kind=kOutput, calls=%fused_computation.55 | convolution fusion | flops 4848353280 | bytes 29921280 | tf_op jit(solution)/shard_map/dot_general | solution.py:58
  433.4 4.5 reduce_max.39
  437.9 0.6 broadcast_divide_fusion
  438.5 20.3 %fusion.8 = (bf16[1536,1536]{1,0:T(8,128)(2,1)}, bf16[1536,1536]{1,0:T(8,128)(2,1)}, f32[1536,1536]{1,0:T(8,128)}) fusion(f32[6,1536]{1,0:T(8,128)S(1)} %get-tuple-element.11, f32[1536,1536]{0,1:T(8,128)} %get-tuple-element.30, f32[6,1536]{1,0:T(8,128)S(1)} %copy-done.4, bf16[1536,1536]{1,0:T(8,128)(2,1)} %param.22, f32[6,1536]{1,0:T(8,128)S(1)} %copy-done.2, ...), kind=kLoop, calls=%fused_computation.15 | loop fusion | flops 56623104 | bytes 42577920 | tf_op jit(solution)/shard_map/convert_element_type | solution.py:53
  458.8 4.5 reduce_max.38
  463.3 0.6 broadcast_divide_fusion.1
  463.9 9.6 %fusion.9 = bf16[1536,1536]{1,0:T(8,128)(2,1)} fusion(f32[6,1536]{1,0:T(8,128)S(1)} %get-tuple-element.13, f32[1536,1536]{0,1:T(8,128)} %get-tuple-element.30, f32[6,1536]{1,0:T(8,128)S(1)} %copy-done.2, bf16[1536,1536]{1,0:T(8,128)(2,1)} %param.20), kind=kLoop, calls=%fused_computation.17 | loop fusion | flops 16515072 | bytes 18948096 | tf_op jit(solution)/shard_map/convert_element_type | solution.py:52
  473.5 0.6 broadcast_divide_fusion.2
  474.2 18.3 %fusion.13 = (bf16[1536,1536]{1,0:T(8,128)(2,1)}, bf16[1536,1536]{1,0:T(8,128)(2,1)}, f32[1536,1536]{1,0:T(8,128)}) fusion(f32[6,1536]{1,0:T(8,128)S(1)} %get-tuple-element.15, f32[1536,1536]{0,1:T(8,128)} %get-tuple-element.28, f32[6,1536]{1,0:T(8,128)S(1)} %copy-done.5, bf16[1536,1536]{1,0:T(8,128)(2,1)} %param.18, f32[6,1536]{1,0:T(8,128)S(1)} %copy-done.3, ...), kind=kLoop, calls=%fused_computation.25 | loop fusion | flops 56623104 | bytes 42577920 | tf_op jit(solution)/shard_map/convert_element_type | solution.py:53
  492.4 4.4 reduce_max.36
  496.8 0.6 broadcast_divide_fusion.3
  497.4 9.8 %fusion.14 = bf16[1536,1536]{1,0:T(8,128)(2,1)} fusion(f32[6,1536]{1,0:T(8,128)S(1)} %get-tuple-element.17, f32[1536,1536]{0,1:T(8,128)} %get-tuple-element.28, f32[6,1536]{1,0:T(8,128)S(1)} %copy-done.3, bf16[1536,1536]{1,0:T(8,128)(2,1)} %param.16), kind=kLoop, calls=%fused_computation.27 | loop fusion | flops 16515072 | bytes 18948096 | tf_op jit(solution)/shard_map/convert_element_type | solution.py:52
  507.3 22.4 %reduce-scatter.5.cloned.1.call-done = f32[768,256]{0,1:T(8,128)} async-done(((f32[6144,256]{0,1:T(8,128)}), f32[768,256]{0,1:T(8,128)}) %reduce-scatter.5.cloned.1.call-update) | async-done | bytes 786448 | tf_op jit(solution)/shard_map/reduce_scatter | solution.py:97
  529.7 1.9 convert_bitcast_fusion
  (14 shorter events, 0.0 us)
Async XLA Ops:
  7.2 66.8 %all-gather.6.cloned.1.call-start = ((), (), s32[]{:S(2)}) async-start(), calls=%async_computation.4 | async-start | bytes 3538944 | tf_op jit(solution)/shard_map/all_gather | solution.py:79
  9.2 126.6 %all-gather.8.cloned.1.call-start = ((), (), s32[]{:S(2)}) async-start(), calls=%async_computation.6 | async-start | bytes 3538944 | tf_op jit(solution)/shard_map/all_gather | solution.py:78
  11.2 184.2 %reduce-scatter.3.cloned.1.call-start = ((), (), s32[]{:S(2)}) async-start(), calls=%async_computation.5 | async-start | bytes 7864320 | tf_op jit(solution)/shard_map/reduce_scatter | solution.py:87
  127.1 189.9 %all-gather.10.cloned.1.call-start = ((), (), s32[]{:S(2)}) async-start(), calls=%async_computation.7 | async-start | bytes 23592960 | tf_op jit(solution)/shard_map/all_gather | solution.py:85
  127.6 276.0 %all-gather.12.cloned.1.call-start = ((), (), s32[]{:S(2)}) async-start(), calls=%async_computation.9 | async-start | bytes 3932160 | tf_op jit(solution)/shard_map/all_gather | solution.py:107
  328.4 92.6 %all-gather.14.cloned.1.call-start = ((), (), s32[]{:S(2)}) async-start(), calls=%async_computation.10 | async-start | bytes 3932160 | tf_op jit(solution)/shard_map/all_gather | solution.py:108
  329.0 11.6 %copy-start = (bf16[256,6144]{0,1:T(8,128)(2,1)S(1)}, bf16[256,6144]{0,1:T(8,128)(2,1)}, u32[]{:S(2)}) copy-start(bf16[256,6144]{0,1:T(8,128)(2,1)} %all-gather.8.cloned.1.call-done) | copy-start | bytes 9437188
  329.0 200.7 %reduce-scatter.5.cloned.1.call-start = ((), (), s32[]{:S(2)}) async-start(), calls=%async_computation.8 | async-start | bytes 7077888 | tf_op jit(solution)/shard_map/reduce_scatter | solution.py:97
  340.5 63.1 %copy-start.5 = (f32[6,1536]{1,0:T(8,128)S(1)}, f32[6,1536]{1,0:T(8,128)}, u32[]{:S(2)}) copy-start(f32[6,1536]{1,0:T(8,128)} %param.19) | copy-start | bytes 110596
  415.9 5.1 copy-start.1
  415.9 5.1 copy-start.4
  433.4 5.1 copy-start.2
  458.7 15.4 %slice-start = ((s8[4718592]{0:T(1024)(128)(4,1)}), s8[524288]{0:T(1024)(128)(4,1)S(1)}, s32[]{:S(2)}) async-start(s8[4718592]{0:T(1024)(128)(4,1)} %bitcast.126), calls=%async_computation.11 | async-start | bytes 1048576
  463.9 10.2 %slice-start.1 = ((s8[4718592]{0:T(1024)(128)(4,1)}), s8[4194304]{0:T(1024)(128)(4,1)S(1)}, s32[]{:S(2)}) async-start(s8[4718592]{0:T(1024)(128)(4,1)} %bitcast.126), calls=%async_computation.12 | async-start | bytes 8388608
  463.9 10.2 %copy-start.3 = (f32[6,1536]{1,0:T(8,128)S(1)}, f32[6,1536]{1,0:T(8,128)}, u32[]{:S(2)}) copy-start(f32[6,1536]{1,0:T(8,128)} %param.17) | copy-start | bytes 110596
Sparse Core Ops, SparseCore 0:
  10.8 63.1 all-gather.5
  76.7 59.0 all-gather.7
  138.3 56.9 reduce-scatter.2
  196.9 120.0 all-gather.9
  328.5 37.0 all-gather.11
  367.7 39.9 all-gather.13
  411.6 117.9 reduce-scatter.4
where the time goes:
time: 539 us; the launch traced here: 538 us
  waiting for transfers between devices  276 us (51%)
  blocking collectives  100 us (19%)
  other arithmetic  80.9 us (15%)
  matrix products  57.2 us (11%)
  between operations  14.2 us (3%)
  local copies, waits for them, and re-layouts  9.84 us (2%)
    all_gather x1, waiting for transfers between devices, local(): up_panel = lax.all_gather(w_expand, 'row', axis=0, tiled=True)  122 us
    all_gather x1, waiting for transfers between devices, local(): lax.all_gather(cotangent, 'col', axis=1, tiled=True)  62.7 us
    all_to_all x1, blocking collectives, local(): lax.all_to_all(token_rows, 'row', split_axis=1, concat_axis=0, tiled=True)  59.8 us
    reduce_scatter x1, waiting for transfers between devices, local(): lax.psum_scatter(jnp.dot(cot_part, w_reduce, preferred_element_type=jnp.f...  59.6 us
    all_to_all x1, blocking collectives, local(): lax.all_to_all(cot_rows, 'row', split_axis=1, concat_axis=0, tiled=True)  40.6 us
    convert_element_type x2, other arithmetic, adam_step(): var_next = spread_scale(var_new, 1.0 / var_scale_next).astype(jnp.bfloat16)  38.5 us
    dot_general x2, matrix products, contract_first(): lax.dot_general(left, right, (((0,), (0,)), ((), ())), preferred_element_...  24.6 us
    reduce_scatter x1, waiting for transfers between devices, local(): lax.psum_scatter(lax.dot_general(up_panel, pre_grad, (((1,), (1,)), ((),...  22.4 us
  transfers between devices with their start and end apart: 7, of which 5 were waited for; matrix products, arithmetic and copies ran while one was open for 25% of the time, Pallas kernels for 0%

commit v1 on v0

v1 whole, which is shorter than its diff:
```python
import functools

import jax
import jax.numpy as jnp
from jax import lax
from jax.experimental import pallas as pl
from jax.experimental.pallas import tpu as pltpu
from jax.sharding import PartitionSpec as P

STEP = 10


beta_one = 0.9
beta_two = 0.999
adam_eps = 1e-08
learn_rate = 0.001
decay_rate = 0.1
scale_eps = 1e-06

MESH = pl.DeviceIdType.MESH
F32 = jnp.float32
BF16 = jnp.bfloat16


def gelu_pair(pre_act):
    cdf_part = 0.5 * (1.0 + lax.erf(pre_act * 0.7071067811865476))
    slope = cdf_part + pre_act * jnp.exp(-0.5 * pre_act * pre_act) * 0.3989422804014327
    return (pre_act * cdf_part, slope)


def ring_place(col, n):
    half, odd = col // 2, col % 2
    return half * (1 - odd) + (n - 1 - half) * odd


def ring_col(place, n):
    place = lax.rem(place + 2 * n, n)
    back = place // (n // 2)
    return (1 - back) * 2 * place + back * (2 * (n - 1 - place) + 1)


def greet(peers):
    barrier = pltpu.get_barrier_semaphore()
    for peer in peers:
        pl.semaphore_signal(barrier, inc=1, device_id=peer, device_id_type=MESH)
    pl.semaphore_wait(barrier, len(peers))


def forward_kernel(
    nrow, ncol,
    tok_ref, cot_ref, we_ref, wr_ref,
    tok_all, cot_all, pg_all, ac_all,
    w_tile, total, send_one, recv_one, send_two, recv_two,
    w_sem, ring_send, ring_recv, one_send, one_recv, two_send, two_recv, out_send, out_recv,
):
    ny = nrow // 2
    half = ncol // 2
    rows = tok_ref.shape[0]
    width = w_tile.shape[3]
    me_c = lax.axis_index("col")
    me_r = lax.axis_index("row")
    y, core = me_r // 2, me_r % 2
    place = ring_place(me_c, ncol)
    right, left = ring_col(place + 1, ncol), ring_col(place - 1, ncol)
    sibling = y * 2 + 1 - core
    others = [lax.rem(y + step, ny) * 2 + core for step in range(1, ny)]

    loads = [
        pltpu.make_async_copy(ref, w_tile.at[i], w_sem.at[i])
        for i, ref in enumerate((we_ref, wr_ref))
    ]
    for load in loads:
        load.start()
    greet([{"col": left}, {"col": right}, {"row": sibling}] + [{"row": o} for o in others])

    gathered = (tok_all, cot_all)
    tok_all[me_c] = tok_ref[...]
    cot_all[me_c] = cot_ref[...]

    def hop(way, step, which, origin):
        slot = ring_col(place + origin, ncol)
        return pltpu.make_async_remote_copy(
            src_ref=gathered[which].at[slot],
            dst_ref=gathered[which].at[slot],
            send_sem=ring_send.at[way, step - 1, which],
            recv_sem=ring_recv.at[way, step - 1, which],
            device_id={"col": right if way == 0 else left},
            device_id_type=MESH,
        )

    def carried(way, step):
        return (0, 1) if step < half else (way,)

    def origin_of(way, distance):
        return -distance if way == 0 else distance

    sent = []
    for which in (0, 1):
        for way in (0, 1):
            if which in carried(way, 1):
                copy = hop(way, 1, which, 0)
                copy.start()
                sent.append(copy)

    tile = width // 3
    total[...] = jnp.zeros_like(total)
    for load in loads:
        load.wait()

    def multiply(which, origin):
        slot = ring_col(place + origin, ncol)
        part, band = slot // nrow, slot % nrow

        @pl.loop(0, 3)
        def _(j):
            cols = pl.ds(pl.multiple_of(j * tile, 128), tile)
            total[which, band, :, cols] += jnp.dot(
                gathered[which][slot], w_tile[which, part, :, cols], preferred_element_type=F32
            )

    multiply(0, 0)
    multiply(1, 0)
    for step in range(1, half + 1):
        for which in (0, 1):
            for way in (0, 1):
                if which in carried(way, step):
                    hop(way, step, which, origin_of(way, step)).wait_recv()
                    if step < half and which in carried(way, step + 1):
                        copy = hop(way, step + 1, which, origin_of(way, step))
                        copy.start()
                        sent.append(copy)
        for which in (0, 1):
            for way in (0, 1):
                if which in carried(way, step):
                    multiply(which, origin_of(way, step))
    for copy in sent:
        copy.wait_send()

    waits = []
    ones = []
    for a in (0, 1):
        for yy in range(ny):
            send_one[a, yy] = total[a, yy * 2 + 1 - core].astype(BF16)
        copy = pltpu.make_async_remote_copy(
            src_ref=send_one.at[a], dst_ref=recv_one.at[a],
            send_sem=one_send.at[a], recv_sem=one_recv.at[a],
            device_id={"row": sibling}, device_id_type=MESH,
        )
        copy.start()
        ones.append(copy)
    twos = []
    for a in (0, 1):
        ones[a].wait_recv()
        for i, other in enumerate(others):
            yt = other // 2
            send_two[a, i] = (total[a, other] + recv_one[a, yt].astype(F32)).astype(BF16)
            copy = pltpu.make_async_remote_copy(
                src_ref=send_two.at[a, i], dst_ref=recv_two.at[a, i],
                send_sem=two_send.at[a, i], recv_sem=two_recv.at[a, i],
                device_id={"row": other}, device_id_type=MESH,
            )
            copy.start()
            twos.append(copy)
        total[a, me_r] = total[a, me_r] + recv_one[a, y].astype(F32)
    for copy in twos:
        copy.wait_recv()

    @pl.loop(0, rows // 16)
    def _(i):
        part = pl.ds(pl.multiple_of(i * 16, 16), 16)
        pre = total[0, me_r, part, :]
        grad = total[1, me_r, part, :]
        for j in range(ny - 1):
            pre = pre + recv_two[0, j, part, :].astype(F32)
            grad = grad + recv_two[1, j, part, :].astype(F32)
        activated, slope = gelu_pair(pre)
        ac_all[me_r, part, :] = activated.astype(BF16)
        pg_all[me_r, part, :] = (grad * slope).astype(BF16)

    outs = (pg_all, ac_all)

    def spread(a, lane, slot, target):
        return pltpu.make_async_remote_copy(
            src_ref=outs[a].at[slot], dst_ref=outs[a].at[slot],
            send_sem=out_send.at[a, lane], recv_sem=out_recv.at[a, lane],
            device_id={"row": target}, device_id_type=MESH,
        )

    last = []
    for a in (0, 1):
        for i, other in enumerate(others):
            copy = spread(a, i, me_r, other)
            copy.start()
            last.append(copy)
    for a in (0, 1):
        copy = spread(a, ny - 1, me_r, sibling)
        copy.start()
        last.append(copy)
    for a in (0, 1):
        for i in range(ny - 1):
            source = lax.rem(y - (i + 1) + ny, ny)
            spread(a, i, source * 2 + core, others[i]).wait_recv()
            copy = spread(a, ny + i, source * 2 + core, sibling)
            copy.start()
            last.append(copy)
    for a in (0, 1):
        spread(a, ny - 1, sibling, sibling).wait_recv()
        for i in range(ny - 1):
            source = lax.rem(y - (i + 1) + ny, ny)
            spread(a, ny + i, source * 2 + 1 - core, sibling).wait_recv()
    for copy in ones + twos + last:
        copy.wait_send()


def forward(tokens, cotangent, w_expand, w_reduce, nrow, ncol):
    rows, wide = tokens.shape
    k, depth, width = w_expand.shape
    ny = nrow // 2
    half = ncol // 2
    any_spec = pl.BlockSpec(memory_space=pl.ANY)
    vmem = pl.BlockSpec(memory_space=pltpu.VMEM)
    dma = pltpu.SemaphoreType.DMA
    return pl.pallas_call(
        functools.partial(forward_kernel, nrow, ncol),
        out_shape=[jax.ShapeDtypeStruct((ncol, rows, wide), BF16)] * 2
        + [jax.ShapeDtypeStruct((nrow, rows, width), BF16)] * 2,
        in_specs=[vmem, vmem, any_spec, any_spec],
        out_specs=[vmem] * 4,
        scratch_shapes=[
            pltpu.VMEM((2, k, depth, width), BF16),
            pltpu.VMEM((2, nrow, rows, width), F32),
            pltpu.VMEM((2, ny, rows, width), BF16),
            pltpu.VMEM((2, ny, rows, width), BF16),
            pltpu.VMEM((2, ny - 1, rows, width), BF16),
            pltpu.VMEM((2, ny - 1, rows, width), BF16),
            dma((2,)),
            dma((2, half, 2)),
            dma((2, half, 2)),
            dma((2,)),
            dma((2,)),
            dma((2, ny - 1)),
            dma((2, ny - 1)),
            dma((2, 2 * ny - 1)),
            dma((2, 2 * ny - 1)),
        ],
        compiler_params=pltpu.CompilerParams(
            collective_id=0, has_side_effects=True, vmem_limit_bytes=58 * 2**20
        ),
        name="forward",
    )(tokens, cotangent, w_expand, w_reduce)


def back_kernel(nrow, ncol, pg_ref, we_ref, out_ref, send, recv, send_sem, recv_sem):
    half = ncol // 2
    rows = out_ref.shape[0]
    mid = rows // 2
    place = ring_place(lax.axis_index("col"), ncol)
    right, left = ring_col(place + 1, ncol), ring_col(place - 1, ncol)
    greet([{"col": left}, {"col": right}])
    halves = (pl.ds(0, mid), pl.ds(mid, mid))

    def partial_sum(offset):
        slot = ring_col(place + offset, ncol)
        return lax.dot_general(
            pg_ref[slot % nrow], we_ref[slot // nrow],
            (((1,), (1,)), ((), ())), preferred_element_type=F32,
        )

    def hop(way, step):
        src, dst = send.at[way, step], recv.at[way, step]
        if step == 0:
            src, dst = src.at[halves[way]], dst.at[halves[way]]
        return pltpu.make_async_remote_copy(
            src_ref=src, dst_ref=dst,
            send_sem=send_sem.at[way, step], recv_sem=recv_sem.at[way, step],
            device_id={"col": right if way == 0 else left}, device_id_type=MESH,
        )

    first = partial_sum(half)
    copies = []
    for way in (0, 1):
        send[way, 0, halves[way], :] = first[way * mid:(way + 1) * mid].astype(BF16)
        copy = hop(way, 0)
        copy.start()
        copies.append(copy)
    for step in range(1, half):
        for way in (0, 1):
            mine = partial_sum(half - step if way == 0 else step - half)
            hop(way, step - 1).wait_recv()
            if step == 1:
                came = mine[way * mid:(way + 1) * mid] + recv[way, 0, halves[way], :].astype(F32)
                send[way, step, halves[way], :] = came.astype(BF16)
                send[way, step, halves[1 - way], :] = mine[
                    (1 - way) * mid:(2 - way) * mid
                ].astype(BF16)
            else:
                send[way, step] = (mine + recv[way, step - 1].astype(F32)).astype(BF16)
            copy = hop(way, step)
            copy.start()
            copies.append(copy)
    mine = partial_sum(0)
    for way in (0, 1):
        hop(way, half - 1).wait_recv()
        mine = mine + recv[way, half - 1].astype(F32)
    out_ref[...] = mine.astype(BF16)
    for copy in copies:
        copy.wait_send()


def backward(pre_grad, w_expand, nrow, ncol):
    rows = pre_grad.shape[1]
    depth = w_expand.shape[1]
    half = ncol // 2
    vmem = pl.BlockSpec(memory_space=pltpu.VMEM)
    dma = pltpu.SemaphoreType.DMA
    return pl.pallas_call(
        functools.partial(back_kernel, nrow, ncol),
        out_shape=jax.ShapeDtypeStruct((rows, depth), BF16),
        in_specs=[vmem, vmem],
        out_specs=vmem,
        scratch_shapes=[
            pltpu.VMEM((2, half, rows, depth), BF16),
            pltpu.VMEM((2, half, rows, depth), BF16),
            dma((2, half)),
            dma((2, half)),
        ],
        compiler_params=pltpu.CompilerParams(
            collective_id=1, has_side_effects=True, vmem_limit_bytes=48 * 2**20
        ),
        name="backward",
    )(pre_grad, w_expand)


def adam_kernel(
    x_ref, g_ref, w_ref, mq_ref, ms_ref, vq_ref, vs_ref,
    nw_ref, mn_ref, msn_ref, vn_ref, vsn_ref,
    grad, mean, var,
):
    row = pl.program_id(1)
    grad[...] = lax.dot_general(
        x_ref[0], g_ref[...], (((0,), (0,)), ((), ())), preferred_element_type=F32
    )
    size, cols = grad.shape
    here = pl.ds(row, 1)
    mean_scale = beta_one * ms_ref[here, :]
    var_scale = beta_two * vs_ref[here, :]
    chunk = 16

    def first(i, tops):
        top_m, top_v = tops
        part = pl.ds(pl.multiple_of(i * chunk, chunk), chunk)
        g = grad[part, :]
        m = mean_scale * mq_ref[part, :].astype(F32) + (1.0 - beta_one) * g
        v = var_scale * vq_ref[part, :].astype(F32) + (1.0 - beta_two) * g * g
        mean[part, :] = m
        var[part, :] = v
        mean_hat = m * (1.0 / (1.0 - beta_one**STEP))
        var_hat = v * (1.0 / (1.0 - beta_two**STEP))
        old = w_ref[part, :].astype(F32)
        step = mean_hat / (jnp.sqrt(var_hat) + adam_eps) + decay_rate * old
        nw_ref[part, :] = (old - learn_rate * step).astype(BF16)
        return jnp.maximum(top_m, jnp.abs(m)), jnp.maximum(top_v, jnp.abs(v))

    zero = jnp.zeros((chunk, cols), F32)
    top_m, top_v = lax.fori_loop(0, size // chunk, first, (zero, zero))
    top_m = jnp.max(top_m, axis=0, keepdims=True) + scale_eps
    top_v = jnp.max(top_v, axis=0, keepdims=True) + scale_eps
    msn_ref[here, :] = top_m
    vsn_ref[here, :] = top_v
    inv_m, inv_v = 1.0 / top_m, 1.0 / top_v

    def second(i, carry):
        part = pl.ds(pl.multiple_of(i * chunk, chunk), chunk)
        mn_ref[part, :] = (mean[part, :] * inv_m).astype(BF16)
        vn_ref[part, :] = (var[part, :] * inv_v).astype(BF16)
        return carry

    lax.fori_loop(0, size // chunk, second, 0)


def adam_step(x, grads, weight, mean_q, mean_scale, var_q, var_scale):
    rows, width = weight.shape
    blocks = mean_scale.shape[0]
    size = rows // blocks
    count = x.shape[1]
    per = x.shape[2] // size
    cols = 512 if width % 512 == 0 else 128
    tile = pl.BlockSpec((size, cols), lambda j, i: (i, j))
    scale = pl.BlockSpec((blocks, cols), lambda j, i: (0, j))
    big = jax.ShapeDtypeStruct((rows, width), BF16)
    small = jax.ShapeDtypeStruct((blocks, width), F32)
    return pl.pallas_call(
        adam_kernel,
        grid=(width // cols, blocks),
        in_specs=[
            pl.BlockSpec((1, count, size), lambda j, i: (i // per, 0, i % per)),
            pl.BlockSpec((count, cols), lambda j, i: (0, j)),
            tile, tile, scale, tile, scale,
        ],
        out_specs=[tile, tile, scale, tile, scale],
        out_shape=[big, big, small, big, small],
        scratch_shapes=[pltpu.VMEM((size, cols), F32)] * 3,
        compiler_params=pltpu.CompilerParams(vmem_limit_bytes=40 * 2**20),
        cost_estimate=pl.CostEstimate(
            flops=2 * count * rows * width, bytes_accessed=14 * rows * width, transcendentals=0
        ),
        name="adam",
    )(x, grads, weight, mean_q, mean_scale, var_q, var_scale)


def local(
    nrow, ncol,
    tokens, cotangent,
    w_expand, w_reduce,
    expand_mean, expand_mean_scale, expand_var, expand_var_scale,
    reduce_mean, reduce_mean_scale, reduce_var, reduce_var_scale,
):
    k = ncol // nrow
    rows, depth = tokens.shape
    width = w_expand.shape[1]
    size = w_expand.shape[0] // expand_mean_scale.shape[0]
    moves = []
    for r in range(nrow):
        for c in range(ncol):
            moves.append((r * ncol + c, (c // k) * ncol + (c % k) * nrow + r))
    returns = [(b, a) for a, b in moves]
    moved_tokens = lax.ppermute(tokens, ("row", "col"), moves)
    moved_cot = lax.ppermute(cotangent, ("row", "col"), moves)
    expand_parts = w_expand.reshape(k, depth, width)
    tok_all, cot_all, pre_grad, activated = forward(
        moved_tokens, moved_cot, expand_parts, w_reduce.reshape(k, depth, width), nrow, ncol
    )
    summed = backward(pre_grad, expand_parts, nrow, ncol)
    grad_tokens = lax.ppermute(summed, ("row", "col"), returns)

    def whole(x):
        x = x.reshape(k, nrow * rows, depth)
        if depth % size:
            x = x.transpose(1, 0, 2).reshape(1, nrow * rows, k * depth)
        return x

    first = adam_step(
        whole(tok_all), pre_grad.reshape(nrow * rows, width), w_expand,
        expand_mean, expand_mean_scale, expand_var, expand_var_scale,
    )
    second = adam_step(
        whole(cot_all), activated.reshape(nrow * rows, width), w_reduce,
        reduce_mean, reduce_mean_scale, reduce_var, reduce_var_scale,
    )
    return (grad_tokens, *first, *second)


def solution(mesh):
    nrow, ncol = mesh.shape["row"], mesh.shape["col"]
    return jax.shard_map(
        functools.partial(local, nrow, ncol),
        mesh=mesh,
        in_specs=(P("row", "col"),) * 12,
        out_specs=(P("row", "col"),) * 11,
        check_vma=False,
    )
```

time: 539 us -> 317 us (0.59)
  Pallas kernels: 0 us -> 302 us
  waiting for transfers between devices: 276 us -> 0.01 us
  blocking collectives: 100 us -> 0 us
  other arithmetic: 80.9 us -> 0.01 us
  matrix products: 57.2 us -> 0 us
  between operations: 14.2 us -> 0.81 us
    pallas_call x0 -> x4, Pallas kernels: none -> 302 us  [the longest x1 202 us: forward(): pl.pallas_call(functools.partial(forward_kernel, nrow, ncol), out_shape=[...]
    all_gather x5 -> x0, waiting for transfers between devices: 192 us -> none  [the longest x1 122 us: local(): up_panel = lax.all_gather(w_expand, 'row', axis=0, tiled=True)]
    all_to_all x2 -> x0, blocking collectives: 100 us -> none  [the longest x1 59.8 us: local(): lax.all_to_all(token_rows, 'row', split_axis=1, concat_axis=0, tiled=True)]
    reduce_scatter x2 -> x0, waiting for transfers between devices: 81.9 us -> none  [the longest x1 59.6 us: local(): lax.psum_scatter(jnp.dot(cot_part, w_reduce, preferred_element_type=jnp.f...]
    convert_element_type x5 -> x0, other arithmetic: 59.9 us -> none  [the longest x2 38.5 us: adam_step(): var_next = spread_scale(var_new, 1.0 / var_scale_next).astype(jnp.bfloat16)]
    dot_general x5 -> x0, matrix products: 57.2 us -> none  [the longest x2 24.6 us: contract_first(): lax.dot_general(left, right, (((0,), (0,)), ((), ())), preferred_element_...]
    reduce_max x4 -> x0, other arithmetic: 18.5 us -> none  [block_max(): return jnp.max(jnp.abs(shaped), axis=1) + scale_eps]
    all_to_all x2 -> x0, local copies, waits for them, and re-layouts: 5.97 us -> none  [the longest x1 3.2 us: local(): lax.all_to_all(token_rows, 'row', split_axis=1, concat_axis=0, tiled=True)]
  transfers between devices with their start and end apart: 7 -> 3, of which waited for: 5 -> 0; matrix products, arithmetic and copies ran while one was open for 25% -> 0% of each run, Pallas kernels for 0% -> 18%
where the time goes in v1:
time: 317 us; the launch traced here: 314 us
  Pallas kernels  302 us (95%)
  local copies, waits for them, and re-layouts  7.45 us (2%)
  starting transfers between devices  3.98 us (1%)
    pallas_call x1, Pallas kernels, forward(): pl.pallas_call(functools.partial(forward_kernel, nrow, ncol), out_shape=[...  202 us
    pallas_call x2, Pallas kernels, adam_step(): pl.pallas_call(adam_kernel, grid=(width // cols, blocks), in_specs=[pl.Bl...  56.8 us
    pallas_call x1, Pallas kernels, backward(): pl.pallas_call(functools.partial(back_kernel, nrow, ncol), out_shape=jax....  43.2 us
    unnamed x29, local copies, waits for them, and re-layouts  7.45 us
  transfers between devices with their start and end apart: 3, of which 0 were waited for; matrix products, arithmetic and copies ran while one was open for 0% of the time, Pallas kernels for 18%

profile of v1, /device:TPU:0, one launch (start us, length us, event | category | flops | bytes accessed | tf_op | source)
XLA Modules:
  0.0 313.9 jit_solution(18164682824912169049)
XLA Ops:
  0.6 1.7 collective-permute-start
  2.3 1.6 collective-permute-start.1
  3.9 0.0 collective-permute-done.tok_ref
  3.9 0.0 copy-start.10
  3.9 0.0 collective-permute-done.1.cot_ref
  4.0 0.0 copy-start.11
  4.0 0.7 copy-done.10
  4.7 0.1 copy-done.11
  4.8 201.7 %forward.1 = (bf16[8,256,768]{2,1,0:T(8,128)(2,1)}, bf16[8,256,768]{2,1,0:T(8,128)(2,1)}, bf16[4,256,1536]{2,1,0:T(8,128)(2,1)}, bf16[4,256,1536]{2,1,0:T(8,128)(2,1)}) custom-call(bf16[256,768]{1,0:T(8,128)(2,1)} %copy-done.10, bf16[256,768]{1,0:T(8,128)(2,1)} %copy-done.11, bf16[2,768,1536]{2,1,0:T(8,128)(2,1)} %bitcast.6, bf16[2,768,1536]{2,1,0:T(8,128)(2,1)} %bitcast.10), custom_call_target="tpu_custom_call" | custom-call | tf_op jit(solution)/shard_map/forward/pallas_call | solution.py:223
  206.5 0.0 copy-start
  206.5 0.0 copy-start.1
  206.5 2.0 copy-done.1
  208.5 0.0 copy-start.6
  208.5 0.0 copy-start.7
  208.5 0.0 slice-start
  208.6 43.2 %backward.1 = bf16[256,768]{1,0:T(8,128)(2,1)S(1)} custom-call(bf16[4,256,1536]{2,1,0:T(8,128)(2,1)S(1)} %copy-done.1, bf16[2,768,1536]{2,1,0:T(8,128)(2,1)} %bitcast.7), custom_call_target="tpu_custom_call" | custom-call | tf_op jit(solution)/shard_map/backward/pallas_call | solution.py:316
  251.8 0.7 collective-permute-start.2
  252.5 0.0 copy-done
  252.5 0.0 copy-done.6
  252.5 0.0 copy-done.7
  252.5 0.0 copy-start.4
  252.5 1.9 copy-done.4
  254.4 0.0 copy-start.5
  254.4 1.9 copy-done.5
  256.3 0.0 slice-start.1
  256.3 0.0 copy-start.2
  256.3 0.0 copy-start.3
  256.3 0.0 copy-start.8
  256.3 0.0 copy-start.9
  256.3 28.7 %adam.3 = (bf16[1536,1536]{1,0:T(8,128)(2,1)}, bf16[1536,1536]{1,0:T(8,128)(2,1)}, f32[6,1536]{1,0:T(8,128)}, bf16[1536,1536]{1,0:T(8,128)(2,1)}, f32[6,1536]{1,0:T(8,128)}) custom-call(bf16[2,1024,768]{2,1,0:T(8,128)(2,1)S(1)} %bitcast.13, bf16[1024,1536]{1,0:T(8,128)(2,1)S(1)} %bitcast.14, bf16[1536,1536]{1,0:T(8,128)(2,1)S(1)} %copy-done, ...), custom_call_target="tpu_custom_call" | custom-call | flops 4831838208 | bytes 33030144 | tf_op jit(solution)/shard_map/adam/pallas_call | solution.py:392
  285.0 0.0 slice-done
  285.0 0.0 slice-done.1
  285.0 0.0 copy-done.2
  285.0 0.0 copy-done.3
  285.0 0.0 copy-done.8
  285.0 0.0 copy-done.9
  285.1 28.1 %adam.2 = (bf16[1536,1536]{1,0:T(8,128)(2,1)}, bf16[1536,1536]{1,0:T(8,128)(2,1)}, f32[6,1536]{1,0:T(8,128)}, bf16[1536,1536]{1,0:T(8,128)(2,1)}, f32[6,1536]{1,0:T(8,128)}) custom-call(bf16[2,1024,768]{2,1,0:T(8,128)(2,1)S(1)} %bitcast.12, bf16[1024,1536]{1,0:T(8,128)(2,1)S(1)} %bitcast.11, bf16[1536,1536]{1,0:T(8,128)(2,1)S(1)} %bitcast.9, ...), custom_call_target="tpu_custom_call" | custom-call | flops 4831838208 | bytes 33030144 | tf_op jit(solution)/shard_map/adam/pallas_call | solution.py:392
  313.2 0.0 collective-permute-done.2
  313.2 0.7 copy.24
  (1 shorter events, 0.0 us)
Async XLA Ops:
  0.6 3.3 %collective-permute-start = (bf16[256,768]{1,0:T(8,128)(2,1)}, bf16[256,768]{1,0:T(8,128)(2,1)S(1)}, u32[]{:S(2)}, u32[]{:S(2)}) collective-permute-start(bf16[256,768]{1,0:T(8,128)(2,1)} %param.12), channel_id=1, source_target_pairs={{0,0},{1,4},{2,8},{3,12},{4,16},{5,20},{6,24},{7,28},{8,1},{9,5},{... | collective-permute-start | bytes 1179656 | tf_op jit(solution)/shard_map/ppermute | solution.py:427
  2.3 1.6 collective-permute-start.1
  3.9 0.7 copy-start.10
  4.0 0.9 copy-start.11
  206.5 46.0 %copy-start = (bf16[1536,1536]{1,0:T(8,128)(2,1)S(1)}, bf16[1536,1536]{1,0:T(8,128)(2,1)}, u32[]{:S(2)}) copy-start(bf16[1536,1536]{1,0:T(8,128)(2,1)} %w_ref.3) | copy-start | bytes 14155780
  206.5 2.0 copy-start.1
  208.5 43.9 %copy-start.6 = (f32[6,1536]{1,0:T(8,128)S(1)}, f32[6,1536]{1,0:T(8,128)}, u32[]{:S(2)}) copy-start(f32[6,1536]{1,0:T(8,128)} %ms_ref.3) | copy-start | bytes 110596
  208.5 44.0 %copy-start.7 = (f32[6,1536]{1,0:T(8,128)S(1)}, f32[6,1536]{1,0:T(8,128)}, u32[]{:S(2)}) copy-start(f32[6,1536]{1,0:T(8,128)} %vs_ref.3) | copy-start | bytes 110596
  208.5 76.4 %slice-start = ((s8[4718592]{0:T(1024)(128)(4,1)}), s8[524288]{0:T(1024)(128)(4,1)S(1)}, s32[]{:S(2)}) async-start(s8[4718592]{0:T(1024)(128)(4,1)} %bitcast.8), calls=%async_computation | async-start | bytes 1048576
  251.8 61.4 %collective-permute-start.2 = (bf16[256,768]{1,0:T(8,128)(2,1)S(1)}, bf16[256,768]{1,0:T(8,128)(2,1)S(1)}, u32[]{:S(2)}, u32[]{:S(2)}) collective-permute-start(bf16[256,768]{1,0:T(8,128)(2,1)S(1)} %backward.1), channel_id=1, source_target_pairs={{0,0},{4,1},{8,2},{12,3},{16,4},{20,5},{24,6},{28,7},{1,8},{5,9},{... | collective-permute-start | bytes 1179656 | tf_op jit(solution)/shard_map/ppermute | solution.py:434
  252.5 1.9 copy-start.4
  254.4 1.9 copy-start.5
  256.3 28.7 %slice-start.1 = ((s8[4718592]{0:T(1024)(128)(4,1)}), s8[4194304]{0:T(1024)(128)(4,1)S(1)}, s32[]{:S(2)}) async-start(s8[4718592]{0:T(1024)(128)(4,1)} %bitcast.8), calls=%async_computation.1 | async-start | bytes 8388608
  256.3 28.7 %copy-start.2 = (bf16[4,256,1536]{2,1,0:T(8,128)(2,1)S(1)}, bf16[4,256,1536]{2,1,0:T(8,128)(2,1)}, u32[]{:S(2)}) copy-start(bf16[4,256,1536]{2,1,0:T(8,128)(2,1)} %get-tuple-element.25.pg_ref) | copy-start | bytes 9437188
  256.3 28.7 %copy-start.3 = (bf16[8,256,768]{2,1,0:T(8,128)(2,1)S(1)}, bf16[8,256,768]{2,1,0:T(8,128)(2,1)}, u32[]{:S(2)}) copy-start(bf16[8,256,768]{2,1,0:T(8,128)(2,1)} %get-tuple-element.26) | copy-start | bytes 9437188
  256.3 28.7 %copy-start.8 = (f32[6,1536]{1,0:T(8,128)S(1)}, f32[6,1536]{1,0:T(8,128)}, u32[]{:S(2)}) copy-start(f32[6,1536]{1,0:T(8,128)} %ms_ref.2) | copy-start | bytes 110596
  256.3 28.7 %copy-start.9 = (f32[6,1536]{1,0:T(8,128)S(1)}, f32[6,1536]{1,0:T(8,128)}, u32[]{:S(2)}) copy-start(f32[6,1536]{1,0:T(8,128)} %vs_ref.2) | copy-start | bytes 110596

commit v2 on v1

v2 whole, which is shorter than its diff:
```python
import functools

import jax
import jax.numpy as jnp
from jax import lax
from jax.experimental import pallas as pl
from jax.experimental.pallas import tpu as pltpu
from jax.sharding import PartitionSpec as P

STEP = 10


beta_one = 0.9
beta_two = 0.999
adam_eps = 1e-08
learn_rate = 0.001
decay_rate = 0.1
scale_eps = 1e-06

MESH = pl.DeviceIdType.MESH
F32 = jnp.float32
BF16 = jnp.bfloat16


def gelu_pair(pre_act):
    cdf_part = 0.5 * (1.0 + lax.erf(pre_act * 0.7071067811865476))
    slope = cdf_part + pre_act * jnp.exp(-0.5 * pre_act * pre_act) * 0.3989422804014327
    return (pre_act * cdf_part, slope)


def ring_place(col, n):
    half, odd = col // 2, col % 2
    return half * (1 - odd) + (n - 1 - half) * odd


def ring_col(place, n):
    place = lax.rem(place + 2 * n, n)
    back = place // (n // 2)
    return (1 - back) * 2 * place + back * (2 * (n - 1 - place) + 1)


def greet(peers):
    barrier = pltpu.get_barrier_semaphore()
    for peer in peers:
        pl.semaphore_signal(barrier, inc=1, device_id=peer, device_id_type=MESH)
    pl.semaphore_wait(barrier, len(peers))


def forward_kernel(
    nrow, ncol,
    tok_ref, cot_ref, we_ref, wr_ref,
    tok_all, cot_all, pg_all, ac_all,
    w_tile, total, recv_one, send_two, recv_two, slope_ref,
    w_sem, ring_send, ring_recv, one_send, one_recv, two_send, two_recv, out_send, out_recv,
):
    ny = nrow // 2
    half = ncol // 2
    rows = tok_ref.shape[0]
    mid = rows // 2
    width = w_tile.shape[3]
    me_c = lax.axis_index("col")
    me_r = lax.axis_index("row")
    y, core = me_r // 2, me_r % 2
    place = ring_place(me_c, ncol)
    right, left = ring_col(place + 1, ncol), ring_col(place - 1, ncol)
    sibling = y * 2 + 1 - core
    others = [lax.rem(y + step, ny) * 2 + core for step in range(1, ny)]
    sources = [lax.rem(y - step + ny, ny) for step in range(1, ny)]

    loads = [
        pltpu.make_async_copy(ref, w_tile.at[i], w_sem.at[i])
        for i, ref in enumerate((we_ref, wr_ref))
    ]
    for load in loads:
        load.start()
    greet([{"col": left}, {"col": right}, {"row": sibling}] + [{"row": o} for o in others])

    gathered = (tok_all, cot_all)
    tok_all[me_c] = tok_ref[...]
    cot_all[me_c] = cot_ref[...]
    sent = []

    def hop(which, way, step, origin):
        block = gathered[which].at[ring_col(place + origin, ncol)]
        if step == half:
            block = block.at[pl.ds(way * mid, mid)]
        return pltpu.make_async_remote_copy(
            src_ref=block,
            dst_ref=block,
            send_sem=ring_send.at[which, way, step - 1],
            recv_sem=ring_recv.at[which, way, step - 1],
            device_id={"col": right if way == 0 else left},
            device_id_type=MESH,
        )

    def launch(copy):
        copy.start()
        sent.append(copy)

    def multiply(which, origin):
        slot = ring_col(place + origin, ncol)
        part, band = slot // nrow, slot % nrow
        tile = width // 3

        @pl.loop(0, 3)
        def _(j):
            cols = pl.ds(pl.multiple_of(j * tile, 128), tile)
            total[which, band, :, cols] += jnp.dot(
                gathered[which][slot], w_tile[which, part, :, cols], preferred_element_type=F32
            )

    def ring_step(which, step, between=None):
        for way in (0, 1):
            origin = -step if way == 0 else step
            hop(which, way, step, origin).wait_recv()
            if step < half:
                launch(hop(which, way, step + 1, origin))
        if between is not None:
            between()
        multiply(which, -step)
        if step < half:
            multiply(which, step)

    def core_swap(a, yy):
        return pltpu.make_async_remote_copy(
            src_ref=total.at[a, yy * 2 + 1 - core], dst_ref=recv_one.at[a, yy],
            send_sem=one_send.at[a, yy], recv_sem=one_recv.at[a, yy],
            device_id={"row": sibling}, device_id_type=MESH,
        )

    def y_swap(a, i):
        return pltpu.make_async_remote_copy(
            src_ref=send_two.at[a, i], dst_ref=recv_two.at[a, i],
            send_sem=two_send.at[a, i], recv_sem=two_recv.at[a, i],
            device_id={"row": others[i]}, device_id_type=MESH,
        )

    def start_cores(a):
        for yy in range(ny):
            launch(core_swap(a, yy))

    def start_y(a):
        for yy in range(ny):
            core_swap(a, yy).wait_recv()
        for i, other in enumerate(others):

            @pl.loop(0, rows // 16)
            def _(n):
                part = pl.ds(pl.multiple_of(n * 16, 16), 16)
                send_two[a, i, part, :] = (
                    total[a, other, part, :] + recv_one[a, other // 2, part, :]
                ).astype(BF16)

            launch(y_swap(a, i))

    def summed(a, part):
        value = total[a, me_r, part, :] + recv_one[a, y, part, :]
        for i in range(ny - 1):
            value = value + recv_two[a, i, part, :].astype(F32)
        return value

    outs = (pg_all, ac_all)

    def spread(a, lane, slot, target):
        return pltpu.make_async_remote_copy(
            src_ref=outs[a].at[slot], dst_ref=outs[a].at[slot],
            send_sem=out_send.at[a, lane], recv_sem=out_recv.at[a, lane],
            device_id={"row": target}, device_id_type=MESH,
        )

    def start_spread(a):
        for i, other in enumerate(others):
            launch(spread(a, i, me_r, other))
        launch(spread(a, ny - 1, me_r, sibling))

    def pass_on(a):
        for i in range(ny - 1):
            slot = sources[i] * 2 + core
            spread(a, i, slot, others[i]).wait_recv()
            launch(spread(a, ny + i, slot, sibling))

    def end_spread(a):
        spread(a, ny - 1, sibling, sibling).wait_recv()
        for i in range(ny - 1):
            spread(a, ny + i, sources[i] * 2 + 1 - core, sibling).wait_recv()

    def activate():
        for i in range(ny - 1):
            y_swap(0, i).wait_recv()

        @pl.loop(0, rows // 16)
        def _(n):
            part = pl.ds(pl.multiple_of(n * 16, 16), 16)
            activated, slope = gelu_pair(summed(0, part))
            ac_all[me_r, part, :] = activated.astype(BF16)
            slope_ref[part, :] = slope

        start_spread(1)

    for way in (0, 1):
        launch(hop(0, way, 1, 0))
    total[...] = jnp.zeros_like(total)
    for load in loads:
        load.wait()
    multiply(0, 0)
    for step in range(1, half + 1):
        if step == half:
            for way in (0, 1):
                launch(hop(1, way, 1, 0))
        ring_step(0, step)
    start_cores(0)
    multiply(1, 0)
    for step in range(1, half + 1):
        if step == half:
            ring_step(1, step, activate)
        elif step == 1:
            ring_step(1, step, lambda: start_y(0))
        else:
            ring_step(1, step)
    start_cores(1)
    start_y(1)
    pass_on(1)
    for i in range(ny - 1):
        y_swap(1, i).wait_recv()

    @pl.loop(0, rows // 16)
    def _(n):
        part = pl.ds(pl.multiple_of(n * 16, 16), 16)
        pg_all[me_r, part, :] = (summed(1, part) * slope_ref[part, :]).astype(BF16)

    start_spread(0)
    pass_on(0)
    end_spread(1)
    end_spread(0)
    for copy in sent:
        copy.wait_send()


def forward(tokens, cotangent, w_expand, w_reduce, nrow, ncol):
    rows, wide = tokens.shape
    k, depth, width = w_expand.shape
    ny = nrow // 2
    half = ncol // 2
    any_spec = pl.BlockSpec(memory_space=pl.ANY)
    vmem = pl.BlockSpec(memory_space=pltpu.VMEM)
    dma = pltpu.SemaphoreType.DMA
    return pl.pallas_call(
        functools.partial(forward_kernel, nrow, ncol),
        out_shape=[jax.ShapeDtypeStruct((ncol, rows, wide), BF16)] * 2
        + [jax.ShapeDtypeStruct((nrow, rows, width), BF16)] * 2,
        in_specs=[vmem, vmem, any_spec, any_spec],
        out_specs=[vmem] * 4,
        scratch_shapes=[
            pltpu.VMEM((2, k, depth, width), BF16),
            pltpu.VMEM((2, nrow, rows, width), F32),
            pltpu.VMEM((2, ny, rows, width), F32),
            pltpu.VMEM((2, ny - 1, rows, width), BF16),
            pltpu.VMEM((2, ny - 1, rows, width), BF16),
            pltpu.VMEM((rows, width), F32),
            dma((2,)),
            dma((2, 2, half)),
            dma((2, 2, half)),
            dma((2, ny)),
            dma((2, ny)),
            dma((2, ny - 1)),
            dma((2, ny - 1)),
            dma((2, 2 * ny - 1)),
            dma((2, 2 * ny - 1)),
        ],
        compiler_params=pltpu.CompilerParams(
            collective_id=0, has_side_effects=True, vmem_limit_bytes=58 * 2**20
        ),
        name="forward",
    )(tokens, cotangent, w_expand, w_reduce)


def backward(pre_grad, w_expand, ncol, beside):
    nrow, rows, _ = pre_grad.shape
    half = ncol // 2
    mid = rows // 2
    place = ring_place(lax.axis_index("col"), ncol)
    cycle = [2 * p if p < half else 2 * (ncol - 1 - p) + 1 for p in range(ncol)]
    rightward = [(cycle[p], cycle[(p + 1) % ncol]) for p in range(ncol)]
    leftward = [(b, a) for a, b in rightward]

    def partial_sum(offset):
        slot = ring_col(place + offset, ncol)
        band = lax.dynamic_index_in_dim(pre_grad, slot % nrow, 0, keepdims=False)
        part = lax.dynamic_index_in_dim(w_expand, slot // nrow, 0, keepdims=False)
        return lax.dot_general(band, part, (((1,), (1,)), ((), ())), preferred_element_type=F32)

    first = partial_sum(half).astype(BF16)
    going = [first[:mid], first[mid:]]
    for step in range(1, half + 1):
        came = [lax.ppermute(going[0], "col", rightward), lax.ppermute(going[1], "col", leftward)]
        came = [x.astype(F32) for x in came]
        if step == 1:
            came = [jnp.pad(came[0], ((0, mid), (0, 0))), jnp.pad(came[1], ((mid, 0), (0, 0)))]
        if step < half:
            mine = beside((partial_sum(half - step), partial_sum(step - half)))
            going = [(m + c).astype(BF16) for m, c in zip(mine, came)]
    (mine,) = beside((partial_sum(0),))
    return (mine + came[0] + came[1]).astype(BF16)


def adam_kernel(
    x_ref, g_ref, w_ref, mq_ref, ms_ref, vq_ref, vs_ref,
    nw_ref, mn_ref, msn_ref, vn_ref, vsn_ref,
    grad, mean, var,
):
    row = pl.program_id(1)
    grad[...] = lax.dot_general(
        x_ref[0], g_ref[...], (((0,), (0,)), ((), ())), preferred_element_type=F32
    )
    size, cols = grad.shape
    here = pl.ds(row, 1)
    mean_scale = beta_one * ms_ref[here, :]
    var_scale = beta_two * vs_ref[here, :]
    chunk = 16

    def first(i, tops):
        top_m, top_v = tops
        part = pl.ds(pl.multiple_of(i * chunk, chunk), chunk)
        g = grad[part, :]
        m = mean_scale * mq_ref[part, :].astype(F32) + (1.0 - beta_one) * g
        v = var_scale * vq_ref[part, :].astype(F32) + (1.0 - beta_two) * g * g
        mean[part, :] = m
        var[part, :] = v
        mean_hat = m * (1.0 / (1.0 - beta_one**STEP))
        var_hat = v * (1.0 / (1.0 - beta_two**STEP))
        old = w_ref[part, :].astype(F32)
        step = mean_hat / (jnp.sqrt(var_hat) + adam_eps) + decay_rate * old
        nw_ref[part, :] = (old - learn_rate * step).astype(BF16)
        return jnp.maximum(top_m, jnp.abs(m)), jnp.maximum(top_v, jnp.abs(v))

    zero = jnp.zeros((chunk, cols), F32)
    top_m, top_v = lax.fori_loop(0, size // chunk, first, (zero, zero))
    top_m = jnp.max(top_m, axis=0, keepdims=True) + scale_eps
    top_v = jnp.max(top_v, axis=0, keepdims=True) + scale_eps
    msn_ref[here, :] = top_m
    vsn_ref[here, :] = top_v
    inv_m, inv_v = 1.0 / top_m, 1.0 / top_v

    def second(i, carry):
        part = pl.ds(pl.multiple_of(i * chunk, chunk), chunk)
        mn_ref[part, :] = (mean[part, :] * inv_m).astype(BF16)
        vn_ref[part, :] = (var[part, :] * inv_v).astype(BF16)
        return carry

    lax.fori_loop(0, size // chunk, second, 0)


def adam_piece(state, begin, number, outs, carried):
    x, grads, weight, mean_q, mean_scale = state[:5]
    rows, width = weight.shape
    blocks = mean_scale.shape[0]
    size = rows // blocks
    count = x.shape[1]
    per = x.shape[2] // size
    cols = adam_cols(width)
    big = jax.ShapeDtypeStruct((rows, width), BF16)
    small = jax.ShapeDtypeStruct((blocks, width), F32)
    tile = pl.BlockSpec((size, cols), lambda j, i: (i, j + begin))
    scale = pl.BlockSpec((blocks, cols), lambda j, i: (0, j + begin))
    held = (*outs, *carried)
    anywhere = pl.BlockSpec(memory_space=pl.ANY)
    first_out = 0 if outs else 5

    def body(*refs):
        start = 7 + len(held)
        adam_kernel(*refs[:7], *refs[start:start + 5], *refs[-3:])

    result = pl.pallas_call(
        body,
        grid=(number, blocks),
        in_specs=[
            pl.BlockSpec((1, count, size), lambda j, i: (i // per, 0, i % per)),
            pl.BlockSpec((count, cols), lambda j, i: (0, j + begin)),
            tile, tile, scale, tile, scale,
        ] + [anywhere] * len(held),
        out_specs=[tile, tile, scale, tile, scale] + [anywhere] * len(carried),
        out_shape=[big, big, small, big, small]
        + [jax.ShapeDtypeStruct(c.shape, c.dtype) for c in carried],
        scratch_shapes=[pltpu.VMEM((size, cols), F32)] * 3,
        input_output_aliases={7 + i: first_out + i for i in range(len(held))},
        compiler_params=pltpu.CompilerParams(vmem_limit_bytes=40 * 2**20),
        cost_estimate=pl.CostEstimate(
            flops=2 * count * rows * cols * number,
            bytes_accessed=14 * rows * cols * number,
            transcendentals=0,
        ),
        name="adam",
    )(*state, *held)
    return tuple(result[:5]), tuple(result[5:])


def adam_cols(width):
    return 512 if width % 512 == 0 else 128


def local(
    nrow, ncol,
    tokens, cotangent,
    w_expand, w_reduce,
    expand_mean, expand_mean_scale, expand_var, expand_var_scale,
    reduce_mean, reduce_mean_scale, reduce_var, reduce_var_scale,
):
    k = ncol // nrow
    rows, depth = tokens.shape
    width = w_expand.shape[1]
    size = w_expand.shape[0] // expand_mean_scale.shape[0]
    moves = []
    for r in range(nrow):
        for c in range(ncol):
            moves.append((r * ncol + c, (c // k) * ncol + (c % k) * nrow + r))
    returns = [(b, a) for a, b in moves]
    moved_tokens = lax.ppermute(tokens, ("row", "col"), moves)
    moved_cot = lax.ppermute(cotangent, ("row", "col"), moves)
    expand_parts = w_expand.reshape(k, depth, width)
    tok_all, cot_all, pre_grad, activated = forward(
        moved_tokens, moved_cot, expand_parts, w_reduce.reshape(k, depth, width), nrow, ncol
    )
    def whole(x):
        x = x.reshape(k, nrow * rows, depth)
        if depth % size:
            x = x.transpose(1, 0, 2).reshape(1, nrow * rows, k * depth)
        return x

    states = (
        (
            whole(cot_all), activated.reshape(nrow * rows, width), w_reduce,
            reduce_mean, reduce_mean_scale, reduce_var, reduce_var_scale,
        ),
        (
            whole(tok_all), pre_grad.reshape(nrow * rows, width), w_expand,
            expand_mean, expand_mean_scale, expand_var, expand_var_scale,
        ),
    )
    tiles = width // adam_cols(width)
    done = [(), ()]
    pieces = [(0, j, 1) for j in range(tiles)] + [(1, 0, 1), (1, 1, tiles - 1)]

    def run_piece(carried):
        which, begin, number = pieces.pop(0)
        done[which], carried = adam_piece(states[which], begin, number, done[which], carried)
        return carried

    def beside(carried):
        return run_piece(carried) if len(pieces) > 1 else carried

    summed = backward(pre_grad, expand_parts, ncol, beside)
    grad_tokens = lax.ppermute(summed, ("row", "col"), returns)
    while pieces:
        run_piece(())
    second, first = done
    return (grad_tokens, *first, *second)


def solution(mesh):
    nrow, ncol = mesh.shape["row"], mesh.shape["col"]
    return jax.shard_map(
        functools.partial(local, nrow, ncol),
        mesh=mesh,
        in_specs=(P("row", "col"),) * 12,
        out_specs=(P("row", "col"),) * 11,
        check_vma=False,
    )
```

time: 317 us -> 283 us (0.89)
  Pallas kernels: 302 us -> 241 us
  matrix products: 0 us -> 9.77 us
  starting transfers between devices: 3.98 us -> 12.3 us
  waiting for transfers between devices: 0.01 us -> 7.7 us
    pallas_call x3 -> x5, Pallas kernels: 100 us -> 60.8 us  [adam_piece(): pl.pallas_call(body, grid=(number, blocks), in_specs=[pl.BlockSpec((1, co...]
    pallas_call x1, Pallas kernels: 202 us -> 180 us  [forward(): pl.pallas_call(functools.partial(forward_kernel, nrow, ncol), out_shape=[...]
    dot_general x0 -> x8, matrix products: none -> 9.77 us  [partial_sum(): lax.dot_general(band, part, (((1,), (1,)), ((), ())), preferred_element_t...]
    ppermute x0 -> x8, starting transfers between devices: none -> 8.35 us  [the longest x4 4.57 us: backward(): lax.ppermute(going[1], 'col', leftward)]
    ppermute x0 -> x8, waiting for transfers between devices: none -> 7.69 us  [the longest x4 7.16 us: backward(): lax.ppermute(going[1], 'col', leftward)]
    unnamed x29 -> x33, local copies, waits for them, and re-layouts: 7.45 us -> 5.9 us
  transfers between devices with their start and end apart: 3 -> 11, of which waited for: 0 -> 2; matrix products, arithmetic and copies ran while one was open for 0% -> 3% of each run, Pallas kernels for 18% -> 22%
where the time goes in v2:
time: 283 us; the launch traced here: 280 us
  Pallas kernels  241 us (85%)
  starting transfers between devices  12.3 us (4%)
  matrix products  9.77 us (3%)
  waiting for transfers between devices  7.7 us (3%)
  local copies, waits for them, and re-layouts  5.93 us (2%)
  other arithmetic  3.11 us (1%)
    pallas_call x1, Pallas kernels, forward(): pl.pallas_call(functools.partial(forward_kernel, nrow, ncol), out_shape=[...  180 us
    pallas_call x5, Pallas kernels, adam_piece(): pl.pallas_call(body, grid=(number, blocks), in_specs=[pl.BlockSpec((1, co...  60.8 us
    dot_general x8, matrix products, partial_sum(): lax.dot_general(band, part, (((1,), (1,)), ((), ())), preferred_element_t...  9.77 us
    ppermute x4, waiting for transfers between devices, backward(): lax.ppermute(going[1], 'col', leftward)  7.16 us
    unnamed x33, local copies, waits for them, and re-layouts  5.9 us
  transfers between devices with their start and end apart: 11, of which 2 were waited for; matrix products, arithmetic and copies ran while one was open for 3% of the time, Pallas kernels for 22%

profile of v2, /device:TPU:0, one launch (start us, length us, event | category | flops | bytes accessed | tf_op | source)
XLA Modules:
  0.0 280.5 jit_solution(9562230150808618721)
XLA Ops:
  0.6 1.7 collective-permute-start
  2.3 1.6 collective-permute-start.1
  3.9 0.0 collective-permute-done.tok_ref
  4.0 0.0 copy-start.11
  4.0 0.7 copy-done.10
  4.7 0.1 copy-done.11
  4.8 179.9 %forward.1 = (bf16[8,256,768]{2,1,0:T(8,128)(2,1)}, bf16[8,256,768]{2,1,0:T(8,128)(2,1)}, bf16[4,256,1536]{2,1,0:T(8,128)(2,1)}, bf16[4,256,1536]{2,1,0:T(8,128)(2,1)}) custom-call(bf16[256,768]{1,0:T(8,128)(2,1)} %copy-done.10, bf16[256,768]{1,0:T(8,128)(2,1)} %copy-done.11, bf16[2,768,1536]{2,1,0:T(8,128)(2,1)} %bitcast.59, bf16[2,768,1536]{2,1,0:T(8,128)(2,1)} %bitcast.56), custom_call_target="tpu_custom_call" | custom-call | tf_op jit(solution)/shard_map/forward/pallas_call | solution.py:247
  184.7 2.1 fusion.24
  186.9 1.2 collective-permute-start.2
  188.1 0.9 collective-permute-start.6
  188.9 0.8 fusion.6.refs_13_
  189.8 0.0 slice-start.1
  189.8 0.0 copy-start.6
  189.8 0.0 copy-start.7
  189.8 0.8 fusion.10.refs_8_
  190.6 0.8 fusion.12.refs_7_
  191.5 1.0 copy-done.1
  192.5 0.9 copy-done.2
  193.4 10.4 %adam.6 = (bf16[1536,1536]{1,0:T(8,128)(2,1)}, bf16[1536,1536]{1,0:T(8,128)(2,1)}, f32[6,1536]{1,0:T(8,128)}, bf16[1536,1536]{1,0:T(8,128)(2,1)}, f32[6,1536]{1,...) custom-call(bf16[2,1024,768]{2,1,0:T(8,128)(2,1)S(1)} %bitcast.70, ...), custom_call_target="tpu_custom_call", output_to_operand_aliasing={{5}: (7, {}), {6}: (8, {})} | custom-call | flops 1610612736 | bytes 11010048 | tf_op jit(solution)/shard_map/adam/pallas_call | solution.py:373
  203.8 0.8 fusion.8.refs_12_
  204.6 10.4 %adam.7 = (bf16[1536,1536]{1,0:T(8,128)(2,1)}, bf16[1536,1536]{1,0:T(8,128)(2,1)}, f32[6,1536]{1,0:T(8,128)}, bf16[1536,1536]{1,0:T(8,128)(2,1)}, f32[6,1536]{1,...) custom-call(bf16[2,1024,768]{2,1,0:T(8,128)(2,1)S(1)} %bitcast.71, ...), custom_call_target="tpu_custom_call", output_to_operand_aliasing={{0}: (7, {}), {1}: (8, {}), {2}: (9, {}), {3}: (10, {}), {4... | custom-call | flops 1610612736 | bytes 11010048 | tf_op jit(solution)/shard_map/adam/pallas_call | solution.py:373
  215.0 0.1 add_convert_fusion.3
  215.1 1.3 collective-permute-start.7
  216.3 0.8 fusion.2.refs_13_
  217.1 0.1 add_convert_fusion.6
  217.2 0.9 collective-permute-start.3
  218.1 0.8 fusion.4.refs_12_
  218.9 7.1 %collective-permute-done.7 = bf16[256,768]{1,0:T(8,128)(2,1)S(1)} collective-permute-done((bf16[256,768]{1,0:T(8,128)(2,1)S(1)}, bf16[256,768]{1,0:T(8,128)(2,1)S(1)}, u32[]{:S(2)}, u32[]{:S(2)}) %collective-permute-start.7) | collective-permute-done | bytes 393248 | tf_op jit(solution)/shard_map/ppermute | solution.py:295
  226.0 0.1 add_convert_fusion.2
  226.1 1.3 collective-permute-start.8
  227.3 0.5 collective-permute-done.3
  227.9 0.1 add_convert_fusion.5
  227.9 0.9 collective-permute-start.4
  228.8 10.4 %adam.8 = (bf16[1536,1536]{1,0:T(8,128)(2,1)}, bf16[1536,1536]{1,0:T(8,128)(2,1)}, f32[6,1536]{1,0:T(8,128)}, bf16[1536,1536]{1,0:T(8,128)(2,1)}, f32[6,1536]{1,...) custom-call(bf16[2,1024,768]{2,1,0:T(8,128)(2,1)S(1)} %bitcast.72, ...), custom_call_target="tpu_custom_call", output_to_operand_aliasing={{0}: (7, {}), {1}: (8, {}), {2}: (9, {}), {3}: (10, {}), {4... | custom-call | flops 1610612736 | bytes 11010048 | tf_op jit(solution)/shard_map/adam/pallas_call | solution.py:373
  239.2 0.0 copy-start.8
  239.2 0.0 copy-start.9
  239.2 0.8 add_convert_fusion.1
  240.0 1.2 collective-permute-start.9
  241.2 0.8 add_convert_fusion.4
  242.1 0.8 collective-permute-start.5
  242.9 2.8 %fusion.14.refs_7_ = f32[256,768]{1,0:T(8,128)S(1)} fusion(bf16[2,768,1536]{2,1,0:T(8,128)(2,1)} %bitcast.60, s32[]{:T(128)S(6)} %select_n.147, bf16[4,256,1536]{2,1,0:T(8,128)(2,1)} %get-tuple-element.48, s32[]{:T(128)S(6)} %select_n.145), kind=kOutput, calls=%fused_computation.14 | convolution fusion | flops 603979776 | bytes 3932168 | tf_op jit(solution)/shard_map/dot_general | solution.py:290
  245.8 0.0 copy-start
  245.8 2.3 copy-done
  248.1 10.3 %adam.5 = (bf16[1536,1536]{1,0:T(8,128)(2,1)}, bf16[1536,1536]{1,0:T(8,128)(2,1)}, f32[6,1536]{1,0:T(8,128)}, bf16[1536,1536]{1,0:T(8,128)(2,1)}, f32[6,1536]{1,0:T(8,128)}, /*index=5*/f32[256,768]{1,0:T(8,128)S(1)}) custom-call(bf16[2,1024,768]{2,1,0:T(8,128)(2,1)S(1)} %bitcast.76, ...), custom_call_target="tpu_custom_call", output_to_operand_aliasing={{5}: (7, {})} | custom-call | flops 1610612736 | bytes 11010048 | tf_op jit(solution)/shard_map/adam/pallas_call | solution.py:373
  258.5 1.2 add_convert_fusion
  259.7 0.7 collective-permute-start.10
  260.4 19.3 %adam.9 = (bf16[1536,1536]{1,0:T(8,128)(2,1)}, bf16[1536,1536]{1,0:T(8,128)(2,1)}, f32[6,1536]{1,0:T(8,128)}, bf16[1536,1536]{1,0:T(8,128)(2,1)}, f32[6,1536]{1,0:T(8,128)}) custom-call(bf16[2,1024,768]{2,1,0:T(8,128)(2,1)S(1)} %bitcast.77, ...), custom_call_target="tpu_custom_call", output_to_operand_aliasing={{0}: (7, {}), {1}: (8, {}), {2}: (9, {}), {3}: (10, {}), {4... | custom-call | flops 3221225472 | bytes 22020096 | tf_op jit(solution)/shard_map/adam/pallas_call | solution.py:373
  279.7 0.7 copy.68
  (31 shorter events, 0.1 us)
Async XLA Ops:
  0.6 3.3 %collective-permute-start = (bf16[256,768]{1,0:T(8,128)(2,1)}, bf16[256,768]{1,0:T(8,128)(2,1)S(1)}, u32[]{:S(2)}, u32[]{:S(2)}) collective-permute-start(bf16[256,768]{1,0:T(8,128)(2,1)} %param.12), channel_id=1, source_target_pairs={{0,0},{1,4},{2,8},{3,12},{4,16},{5,20},{6,24},{7,28},{8,1},{9,5},{... | collective-permute-start | bytes 1179656 | tf_op jit(solution)/shard_map/ppermute | solution.py:417
  2.3 1.7 collective-permute-start.1
  3.9 180.8 %slice-start.2 = ((s8[4718592]{0:T(1024)(128)(4,1)}), s8[524288]{0:T(1024)(128)(4,1)S(1)}, s32[]{:S(2)}) async-start(s8[4718592]{0:T(1024)(128)(4,1)} %bitcast.61), calls=%async_computation.2 | async-start | bytes 1048576
  3.9 0.7 copy-start.10
  4.0 0.9 copy-start.11
  4.8 179.9 %slice-start.3 = ((s8[4718592]{0:T(1024)(128)(4,1)}), s8[4194304]{0:T(1024)(128)(4,1)S(1)}, s32[]{:S(2)}) async-start(s8[4718592]{0:T(1024)(128)(4,1)} %bitcast.61), calls=%async_computation.3 | async-start | bytes 8388608
  184.7 4.3 %copy-start.4 = (bf16[4,256,1536]{2,1,0:T(8,128)(2,1)S(1)}, bf16[4,256,1536]{2,1,0:T(8,128)(2,1)}, u32[]{:S(2)}) copy-start(bf16[4,256,1536]{2,1,0:T(8,128)(2,1)} %get-tuple-element.48) | copy-start | bytes 9437188
  186.9 30.3 %collective-permute-start.2 = (bf16[128,768]{1,0:T(8,128)(2,1)S(1)}, bf16[128,768]{1,0:T(8,128)(2,1)S(1)}, u32[]{:S(2)}, u32[]{:S(2)}) collective-permute-start(bf16[128,768]{1,0:T(8,128)(2,1)S(1)} %get-tuple-element.83), channel_id=1, source_target_pairs={{0,2},{2,4},{4,6},{6,7},{7,5},{5,3},{3,1},{1,0},{8,10},{10,12},{12... | collective-permute-start | bytes 589832 | tf_op jit(solution)/shard_map/ppermute | solution.py:295
  188.1 26.9 %collective-permute-start.6 = (bf16[128,768]{1,0:T(8,128)(2,1)S(1)}, bf16[128,768]{1,0:T(8,128)(2,1)S(1)}, u32[]{:S(2)}, u32[]{:S(2)}) collective-permute-start(bf16[128,768]{1,0:T(8,128)(2,1)S(1)} %get-tuple-element.84), channel_id=1, source_target_pairs={{2,0},{4,2},{6,4},{7,6},{5,7},{3,5},{1,3},{0,1},{10,8},{12,10},{14... | collective-permute-start | bytes 589832 | tf_op jit(solution)/shard_map/ppermute | solution.py:295
  188.9 2.5 slice-start
  189.8 1.7 slice-start.1
  189.8 2.7 copy-start.1
  189.8 3.6 %copy-start.2 = (bf16[4,256,1536]{2,1,0:T(8,128)(2,1)S(1)}, bf16[4,256,1536]{2,1,0:T(8,128)(2,1)}, u32[]{:S(2)}) copy-start(bf16[4,256,1536]{2,1,0:T(8,128)(2,1)} %get-tuple-element.51) | copy-start | bytes 9437188
  189.8 3.6 %copy-start.6 = (f32[6,1536]{1,0:T(8,128)S(1)}, f32[6,1536]{1,0:T(8,128)}, u32[]{:S(2)}) copy-start(f32[6,1536]{1,0:T(8,128)} %refs_4_.8) | copy-start | bytes 110596
  189.8 3.6 %copy-start.7 = (f32[6,1536]{1,0:T(8,128)S(1)}, f32[6,1536]{1,0:T(8,128)}, u32[]{:S(2)}) copy-start(f32[6,1536]{1,0:T(8,128)} %refs_6_.8) | copy-start | bytes 110596
  215.1 11.0 %collective-permute-start.7 = (bf16[256,768]{1,0:T(8,128)(2,1)S(1)}, bf16[256,768]{1,0:T(8,128)(2,1)S(1)}, u32[]{:S(2)}, u32[]{:S(2)}) collective-permute-start(bf16[256,768]{1,0:T(8,128)(2,1)S(1)} %add_convert_fusion.3), channel_id=1, source_target_pairs={{2,0},{4,2},{6,4},{7,6},{5,7},{3,5},{1,3},{0,1},{10,8},{12,10},{14... | collective-permute-start | bytes 1179656 | tf_op jit(solution)/shard_map/ppermute | solution.py:295
  217.2 10.7 %collective-permute-start.3 = (bf16[256,768]{1,0:T(8,128)(2,1)S(1)}, bf16[256,768]{1,0:T(8,128)(2,1)S(1)}, u32[]{:S(2)}, u32[]{:S(2)}) collective-permute-start(bf16[256,768]{1,0:T(8,128)(2,1)S(1)} %add_convert_fusion.6), channel_id=1, source_target_pairs={{0,2},{2,4},{4,6},{6,7},{7,5},{5,3},{3,1},{1,0},{8,10},{10,12},{12... | collective-permute-start | bytes 1179656 | tf_op jit(solution)/shard_map/ppermute | solution.py:295
  226.1 13.1 %collective-permute-start.8 = (bf16[256,768]{1,0:T(8,128)(2,1)S(1)}, bf16[256,768]{1,0:T(8,128)(2,1)S(1)}, u32[]{:S(2)}, u32[]{:S(2)}) collective-permute-start(bf16[256,768]{1,0:T(8,128)(2,1)S(1)} %add_convert_fusion.2), channel_id=1, source_target_pairs={{2,0},{4,2},{6,4},{7,6},{5,7},{3,5},{1,3},{0,1},{10,8},{12,10},{14... | collective-permute-start | bytes 1179656 | tf_op jit(solution)/shard_map/ppermute | solution.py:295
  227.9 13.3 %collective-permute-start.4 = (bf16[256,768]{1,0:T(8,128)(2,1)S(1)}, bf16[256,768]{1,0:T(8,128)(2,1)S(1)}, u32[]{:S(2)}, u32[]{:S(2)}) collective-permute-start(bf16[256,768]{1,0:T(8,128)(2,1)S(1)} %add_convert_fusion.5), channel_id=1, source_target_pairs={{0,2},{2,4},{4,6},{6,7},{7,5},{5,3},{3,1},{1,0},{8,10},{10,12},{12... | collective-permute-start | bytes 1179656 | tf_op jit(solution)/shard_map/ppermute | solution.py:295
  239.2 6.6 %copy-start.3 = (bf16[8,256,768]{2,1,0:T(8,128)(2,1)S(1)}, bf16[8,256,768]{2,1,0:T(8,128)(2,1)}, u32[]{:S(2)}) copy-start(bf16[8,256,768]{2,1,0:T(8,128)(2,1)} %get-tuple-element.47) | copy-start | bytes 9437188
  239.2 6.6 %copy-start.8 = (f32[6,1536]{1,0:T(8,128)S(1)}, f32[6,1536]{1,0:T(8,128)}, u32[]{:S(2)}) copy-start(f32[6,1536]{1,0:T(8,128)} %refs_4_.9) | copy-start | bytes 110596
  239.2 6.6 %copy-start.9 = (f32[6,1536]{1,0:T(8,128)S(1)}, f32[6,1536]{1,0:T(8,128)}, u32[]{:S(2)}) copy-start(f32[6,1536]{1,0:T(8,128)} %refs_6_.9) | copy-start | bytes 110596
  240.0 18.4 %collective-permute-start.9 = (bf16[256,768]{1,0:T(8,128)(2,1)}, bf16[256,768]{1,0:T(8,128)(2,1)}, u32[]{:S(2)}, u32[]{:S(2)}) collective-permute-start(bf16[256,768]{1,0:T(8,128)(2,1)} %add_convert_fusion.1), channel_id=1, source_target_pairs={{2,0},{4,2},{6,4},{7,6},{5,7},{3,5},{1,3},{0,1},{10,8},{12,10},{14... | collective-permute-start | bytes 1179656 | tf_op jit(solution)/shard_map/ppermute | solution.py:295
  242.1 16.4 %collective-permute-start.5 = (bf16[256,768]{1,0:T(8,128)(2,1)}, bf16[256,768]{1,0:T(8,128)(2,1)}, u32[]{:S(2)}, u32[]{:S(2)}) collective-permute-start(bf16[256,768]{1,0:T(8,128)(2,1)} %add_convert_fusion.4), channel_id=1, source_target_pairs={{0,2},{2,4},{4,6},{6,7},{7,5},{5,3},{3,1},{1,0},{8,10},{10,12},{12... | collective-permute-start | bytes 1179656 | tf_op jit(solution)/shard_map/ppermute | solution.py:295
  242.9 2.9 %copy-start.5 = (bf16[4,256,1536]{2,1,0:T(8,128)(2,1)S(1)}, bf16[4,256,1536]{2,1,0:T(8,128)(2,1)}, u32[]{:S(2)}) copy-start(bf16[4,256,1536]{2,1,0:T(8,128)(2,1)} %get-tuple-element.48) | copy-start | bytes 9437188
  245.8 2.3 copy-start
  259.7 20.0 %collective-permute-start.10 = (bf16[256,768]{1,0:T(8,128)(2,1)S(1)}, bf16[256,768]{1,0:T(8,128)(2,1)S(1)}, u32[]{:S(2)}, u32[]{:S(2)}) collective-permute-start(bf16[256,768]{1,0:T(8,128)(2,1)S(1)} %add_convert_fusion), channel_id=1, source_target_pairs={{0,0},{4,1},{8,2},{12,3},{16,4},{20,5},{24,6},{28,7},{1,8},{5,9},{... | collective-permute-start | bytes 1179656 | tf_op jit(solution)/shard_map/ppermute | solution.py:452
